TPU v7x, 256 devices: a whole 4x4x8 slice. The times are simulated.
256 devices in a mesh: lat: 16 (over y_lo, x, core), lon: 16 (over z, y_hi).
Axes of the slice: x: 4, y: 4 (y_hi: 2, y_lo: 2; y = y_hi * 2 + y_lo), z: 8, core: 2. Of those that a mesh axis runs over, the one named last changes fastest.
Arguments:
- nodes: bfloat16 [64, 32, 128, 512], P('lat', 'lon'), may hold values from -6 to 6
- neighbours: int32 [64, 32, 12], P('lat', 'lon'), may hold values from 0 to 2047, as said below
- live: int32 [64, 32], P('lat', 'lon'), may hold values from 6 to 12
- gain_attn: float32 [512], replicated, may hold values from 0.25 to 1.75
- w_query: bfloat16 [512, 512], replicated, may hold values from -2 to 2
- w_key: bfloat16 [512, 512], replicated, may hold values from -2 to 2
- w_value: bfloat16 [512, 512], replicated, may hold values from -0.25 to 0.25
- w_out: bfloat16 [512, 512], replicated, may hold values from -0.25 to 0.25
- gain_mlp: float32 [512], replicated, may hold values from 0.25 to 1.75
- w_in: bfloat16 [512, 2048], replicated, may hold values from -0.25 to 0.25
- w_back: bfloat16 [2048, 512], replicated, may hold values from -0.125 to 0.125
Outputs:
- updated: bfloat16 [64, 32, 128, 512], P('lat', 'lon')
Inputs may be any that keep to these rules, and one draw needn't show every extreme that they name: `neighbours`: slot 0 of each block is the block itself; slots below live name distinct blocks; every named block lies at most 1 block row and at most 2 block columns away, columns counted around the sphere modulo 32, and inside rows 0 to 63.
All inputs are finite; a program needn't handle non-finite values.
Results may differ from a plain program's by a relative error of at most 0.006.
Values may be sent and summed in bfloat16 or wider, within the bound.
No kernel may reach another device: no remote copies, remote signals or barrier semaphores. Data moves between devices by JAX's collectives and lax.ppermute only.
A program may use at most 128 MiB of HBM per device.

v0:
```python
import math

import jax
import jax.numpy as jnp
from jax import lax
from jax.sharding import PartitionSpec as P

HEADS = 8
NBR = 12


def from_behind(value, axis, steps):
    count = lax.axis_size(axis)
    pairs = [(source, (source + steps) % count) for source in range(count)]
    return lax.ppermute(value, axis, pairs)


def passed_along(value, axis, by):
    size = lax.axis_size(axis)
    pairs = [(i, i + by) for i in range(size) if 0 <= i + by < size]
    return lax.ppermute(value, axis, pairs)


def normalize(values, gain):
    centre = values - jnp.mean(values, axis=-1, keepdims=True)
    spread = jnp.mean(centre * centre, axis=-1, keepdims=True)
    return centre * lax.rsqrt(spread + 1e-05) * gain


def lon_piece(part, step):
    return from_behind(part, "lon", step)


def lat_piece(part, step):
    return passed_along(part, "lat", step)


def widen_lon(field):
    return jnp.concatenate([lon_piece(field, 1), field, lon_piece(field, -1)], axis=1)


def widen_lat(field):
    return jnp.concatenate([lat_piece(field[-1:], 1), field, lat_piece(field[:1], -1)], axis=0)


def shards(
    nodes, neighbours, live, gain_attn, w_query, w_key, w_value, w_out, gain_mlp, w_in, w_back
):
    rows, cols, nblk, width = nodes.shape
    blocks = rows * cols
    head_dim = width // HEADS
    flat = nodes.astype(jnp.float32).reshape(-1, width)
    normed = normalize(flat, gain_attn).astype(jnp.bfloat16)
    query = jnp.dot(normed, w_query, preferred_element_type=jnp.float32).astype(jnp.bfloat16)
    shaped = normed.reshape(rows, cols, nblk, width)
    plain = shaped.reshape(-1, width)
    keys = jnp.dot(plain, w_key, preferred_element_type=jnp.float32).astype(jnp.bfloat16)
    values = jnp.dot(plain, w_value, preferred_element_type=jnp.float32).astype(jnp.bfloat16)
    source = jnp.concatenate([keys, values], axis=-1).reshape(shaped.shape[:-1] + (2 * width,))
    extended = widen_lat(widen_lon(source))
    extended = extended.reshape(-1, nblk, 2 * width)
    total_lon = cols * lax.axis_size("lon")
    lat_start = lax.axis_index("lat") * rows
    lon_start = lax.axis_index("lon") * cols
    glat = neighbours // total_lon
    glon = neighbours % total_lon
    local = (glat - lat_start + 1) * (cols + 4) + (glon - lon_start + 2) % total_lon
    group = math.gcd(blocks, 4)
    local = local.reshape(blocks // group, group, NBR)
    counts = live.reshape(blocks // group, group)
    qgroups = query.reshape(blocks // group, group, nblk, width)
    nkeys = NBR * nblk
    slots = jnp.arange(nkeys, dtype=jnp.int32) // nblk

    def attend_group(args):
        qg, ig, cg = args
        gathered = extended[ig].reshape(group, nkeys, 2 * width)
        qh = qg.reshape(group, nblk, HEADS, head_dim)
        kh = gathered[..., :width].reshape(group, nkeys, HEADS, head_dim)
        vh = gathered[..., width:].reshape(group, nkeys, HEADS, head_dim)
        scores = jnp.einsum("gqhd,gkhd->ghqk", qh, kh, preferred_element_type=jnp.float32) * (
            1.0 / head_dim**0.5
        )
        usable = slots[None, :] < cg[:, None]
        scores = jnp.where(usable[:, None, None, :], scores, jnp.float32(-1e30))
        top = jnp.max(scores, axis=-1, keepdims=True)
        expo = jnp.exp(scores - top)
        weights = (expo / jnp.sum(expo, axis=-1, keepdims=True)).astype(jnp.bfloat16)
        out = jnp.einsum("ghqk,gkhd->gqhd", weights, vh, preferred_element_type=jnp.float32)
        return out.astype(jnp.bfloat16).reshape(group, nblk, width)

    attended = lax.map(attend_group, (qgroups, local, counts)).reshape(-1, width)
    mid = flat + jnp.dot(attended, w_out, preferred_element_type=jnp.float32)
    second = normalize(mid, gain_mlp).astype(jnp.bfloat16)
    inner = jax.nn.gelu(
        jnp.dot(second, w_in, preferred_element_type=jnp.float32), approximate=True
    ).astype(jnp.bfloat16)
    updated = mid + jnp.dot(inner, w_back, preferred_element_type=jnp.float32)
    return updated.astype(jnp.bfloat16).reshape(rows, cols, nblk, width)


def solution(mesh):
    placed = (
        P("lat", "lon", None, None),
        P("lat", "lon", None),
        P("lat", "lon"),
        P(),
        P(),
        P(),
        P(),
        P(),
        P(),
        P(),
        P(),
    )
    return jax.shard_map(
        shards, mesh=mesh, in_specs=placed, out_specs=P("lat", "lon", None, None), check_vma=False
    )
```

profile of v0, /device:TPU:6, one launch (start us, length us, event | category | flops | bytes accessed | tf_op | source)
XLA Modules:
  0.0 313.5 jit_solution(1840221063447701817)
XLA Ops:
  0.0 0.0 copy-start
  0.0 0.0 copy-start.7
  0.0 0.0 copy-start.8
  0.0 1.6 convert_reduce_fusion
  1.6 1.7 fusion.33
  3.3 1.6 fusion.36
  5.0 0.0 copy-done.7
  5.0 0.8 convolution_convert_fusion.1
  5.7 0.0 copy-done.8
  5.8 0.8 convolution_convert_fusion.2
  6.5 1.5 pad_maximum_fusion.1
  8.0 4.0 %copy.31 = bf16[1024,1024]{1,0:T(8,128)(2,1)} copy(bf16[1024,1024]{0,1:T(8,128)(2,1)} %pad_maximum_fusion.1) | data formatting | bytes 4194304 | tf_op jit(solution)/shard_map/reshape | solution.py:59
  12.0 0.0 copy-start.6
  12.0 3.2 %collective-permute-start = (bf16[4,2,128,1024]{3,2,1,0:T(8,128)(2,1)}, bf16[4,2,128,1024]{3,2,1,0:T(8,128)(2,1)S(1)}, u32[]{:S(2)}, u32[]{:S(2)}) collective-permute-start(bf16[4,2,128,1024]{3,2,1,0:T(8,128)(2,1)} %bitcast.76), channel_id=1, source_target_pairs={{0,1},{1,2},{2,3},{3,4},{4,5},{5,6},{6,7},{7,8},{8,9},{9,10},{10,1... | collective-permute-start | bytes 6291464 | tf_op jit(solution)/shard_map/ppermute | solution.py:15
  15.2 5.4 %collective-permute-start.1 = (bf16[4,2,128,1024]{3,2,1,0:T(8,128)(2,1)}, bf16[4,2,128,1024]{3,2,1,0:T(8,128)(2,1)S(1)}, u32[]{:S(2)}, u32[]{:S(2)}) collective-permute-start(bf16[4,2,128,1024]{3,2,1,0:T(8,128)(2,1)} %bitcast.77), channel_id=1, source_target_pairs={{0,15},{1,0},{2,1},{3,2},{4,3},{5,4},{6,5},{7,6},{8,7},{9,8},{10,9... | collective-permute-start | bytes 6291464 | tf_op jit(solution)/shard_map/ppermute | solution.py:15
  20.5 84.8 %collective-permute-done = bf16[4,2,128,1024]{3,2,1,0:T(8,128)(2,1)S(1)} collective-permute-done((bf16[4,2,128,1024]{3,2,1,0:T(8,128)(2,1)}, bf16[4,2,128,1024]{3,2,1,0:T(8,128)(2,1)S(1)}, u32[]{:S(2)}, u32[]{:S(2)}) %collective-permute-start) | collective-permute-done | bytes 2097184 | tf_op jit(solution)/shard_map/ppermute | solution.py:15
  105.3 3.6 %collective-permute-done.1 = bf16[4,2,128,1024]{3,2,1,0:T(8,128)(2,1)S(1)} collective-permute-done((bf16[4,2,128,1024]{3,2,1,0:T(8,128)(2,1)}, bf16[4,2,128,1024]{3,2,1,0:T(8,128)(2,1)S(1)}, u32[]{:S(2)}, u32[]{:S(2)}) %collective-permute-start.1) | collective-permute-done | bytes 2097184 | tf_op jit(solution)/shard_map/ppermute | solution.py:15
  108.9 3.3 %pad_maximum_fusion.4 = (bf16[1,6,128,1024]{3,2,1,0:T(8,128)(2,1)}, bf16[1,6,128,1024]{3,2,1,0:T(8,128)(2,1)}) fusion(bf16[4,2,128,1024]{3,2,1,0:T(8,128)(2,1)S(1)} %collective-permute-done.1, bf16[4,2,128,1024]{3,2,1,0:T(8,128)(2,1)} %bitcast.78, bf16[4,2,128,1024]{3,2,1,0:T(8,128)(2,1)S(1)} %collective-permute-done), kind=kLoop, calls=%fused_computation.59 | loop fusion | flops 3145728 | bytes 9437184 | tf_op jit(solution)/shard_map/slice | solution.py:43
  112.2 0.0 copy-done.2
  112.2 0.0 copy-done.3
  112.2 1.9 collective-permute-start.2
  114.1 3.6 %collective-permute-start.3 = (bf16[1,6,128,1024]{3,2,1,0:T(8,128)(2,1)}, bf16[1,6,128,1024]{3,2,1,0:T(8,128)(2,1)}, u32[]{:S(2)}, u32[]{:S(2)}) collective-permute-start(bf16[1,6,128,1024]{3,2,1,0:T(8,128)(2,1)} %get-tuple-element.90), channel_id=1, source_target_pairs={{16,0},{32,16},{48,32},{64,48},{80,64},{96,80},{112,96},{128,112},... | collective-permute-start | bytes 4718600 | tf_op jit(solution)/shard_map/ppermute | solution.py:21
  117.8 0.0 copy-done.6
  117.8 0.1 copy.28
  117.9 0.1 reshape.146
  117.9 0.0 copy-done.5
  118.0 2.9 convolution_convert_fusion
  120.9 13.3 %collective-permute-done.2 = bf16[1,6,128,1024]{3,2,1,0:T(8,128)(2,1)} collective-permute-done((bf16[1,6,128,1024]{3,2,1,0:T(8,128)(2,1)}, bf16[1,6,128,1024]{3,2,1,0:T(8,128)(2,1)}, u32[]{:S(2)}, u32[]{:S(2)}) %collective-permute-start.2) | collective-permute-done | bytes 1572896 | tf_op jit(solution)/shard_map/ppermute | solution.py:21
  134.2 1.8 collective-permute-done.3
  136.0 0.0 copy-done.1
  136.0 7.3 %pad_maximum_fusion = bf16[6,6,128,1024]{3,2,1,0:T(8,128)(2,1)} fusion(bf16[1,6,128,1024]{3,2,1,0:T(8,128)(2,1)} %collective-permute-done.3, bf16[4,2,128,1024]{3,2,1,0:T(8,128)(2,1)} %copy-done.3, bf16[4,2,128,1024]{3,2,1,0:T(8,128)(2,1)S(1)} %bitcast.79, bf16[4,2,128,1024]{3,2,1,0:T(8,128)(2,1)} %copy-done.2, ...), kind=kLoop, calls=%fused_computation.33 | loop fusion | flops 18874368 | bytes 18874368 | tf_op jit(solution)/shard_map/concatenate | solution.py:43
  143.3 157.3 %while.11 = (s32[]{:T(128)}, bf16[2,4,128,512]{3,2,1,0:T(8,128)(2,1)}, s32[2,4,12]{2,1,0:T(4,128)S(1)}, bf16[36,128,1024]{2,1,0:T(8,128)(2,1)}, s32[2,4]{1,0:T(2...) while((s32[]{:T(128)}, bf16[2,4,128,512]{3,2,1,0:T(8,128)(2,1)}, ...), condition=%wide.region_5.6_spmd.clone, body=%wide.region_2.5_spmd.clone.sunk | while | flops 2472830976 | bytes 150540048 | solution.py:92
  143.3 0.1 reshape.172
  143.4 10.0 %gather_fusion = bf16[48,128,1024]{2,1,0:T(8,128)(2,1)} fusion(bf16[36,128,1024]{2,1,0:T(8,128)(2,1)} %get-tuple-element.151, s32[1024]{0:T(1024)S(1)} %pad_clamp_fusion.2), kind=kCustom, calls=%fused_computation.clone.clone.1 | custom fusion | bytes 25166016 | tf_op jit(solution)/shard_map/while/body/eval_jaxpr/gather | solution.py:77
  153.4 10.3 %fusion.88 = (bf16[4,1536,512]{2,1,0:T(8,128)(2,1)}, bf16[4,1536,512]{2,1,0:T(8,128)(2,1)}) fusion(bf16[4,1536,1024]{2,1,0:T(8,128)(2,1)} %bitcast.69), kind=kLoop, calls=%fused_computation.85.clone.1 | loop fusion | bytes 25165824 | tf_op jit(solution)/shard_map/while/body/eval_jaxpr/slice | solution.py:79
  163.7 8.6 %copy.43 = bf16[4,1536,512]{1,2,0:T(8,128)(2,1)} copy(bf16[4,1536,512]{2,1,0:T(8,128)(2,1)} %get-tuple-element.133) | data formatting | bytes 12582912 | tf_op jit(solution)/shard_map/while
  172.3 1.1 constant_dynamic-slice_fusion.3
  173.4 0.3 copy.42
  173.7 0.1 broadcast_compare_fusion.2
  173.8 9.8 %fusion.90 = f32[4,8,128]{2,1,0:T(8,128)S(1)} fusion(pred[4,1536]{1,0:T(4,128)(4,1)S(1)} %broadcast_compare_fusion.2, bf16[4,128,8,64]{1,3,2,0:T(8,128)(2,1)S(1)} %bitcast.74, bf16[4,1536,8,64]{1,3,2,0:T(8,128)(2,1)} %bitcast.70), kind=kOutput, calls=%fused_computation.86.clone.1 | convolution fusion | flops 830473728 | bytes 6838272 | tf_op jit(solution)/shard_map/while/body/eval_jaxpr/sub | solution.py:87
  183.6 14.5 %fusion.91 = f32[4,8,128,1536]{3,2,1,0:T(8,128)} fusion(bf16[4,128,8,64]{1,3,2,0:T(8,128)(2,1)S(1)} %bitcast.75, bf16[4,1536,8,64]{1,3,2,0:T(8,128)(2,1)} %bitcast.71), kind=kOutput, calls=%fused_computation.88.clone.1 | convolution fusion | flops 805306368 | bytes 31981568 | tf_op jit(solution)/shard_map/while/body/eval_jaxpr/gqhd,gkhd->ghqk/dot_general | solution.py:81
  198.1 8.6 %copy.41 = bf16[4,1536,512]{1,2,0:T(8,128)(2,1)} copy(bf16[4,1536,512]{2,1,0:T(8,128)(2,1)} %get-tuple-element.132) | data formatting | bytes 12582912 | tf_op jit(solution)/shard_map/while
  206.8 14.1 %fusion.92 = bf16[4,8,64,128]{3,2,1,0:T(8,128)(2,1)S(1)} fusion(bf16[4,1536,8,64]{1,3,2,0:T(8,128)(2,1)} %bitcast.73, f32[4,8,128]{2,1,0:T(8,128)S(1)} %fusion.90, f32[4,8,128,1536]{3,2,1,0:T(8,128)} %fusion.91, pred[4,1536]{1,0:T(4,128)(4,1)S(1)} %broadcast_compare_fusion.2), kind=kOutput, calls=%fused_computation.12.clone.1 | convolution fusion | flops 837031424 | bytes 32004096 | tf_op jit(solution)/shard_map/while/body/eval_jaxpr/ghqk,gkhd->gqhd/dot_general | solution.py:89
  220.9 0.2 copy.44
  221.1 0.8 constant_dynamic-update-slice_fusion.2
  221.9 0.1 reshape.172
  222.0 10.0 %gather_fusion = bf16[48,128,1024]{2,1,0:T(8,128)(2,1)} fusion(bf16[36,128,1024]{2,1,0:T(8,128)(2,1)} %get-tuple-element.151, s32[1024]{0:T(1024)S(1)} %pad_clamp_fusion.2), kind=kCustom, calls=%fused_computation.clone.clone.1 | custom fusion | bytes 25166016 | tf_op jit(solution)/shard_map/while/body/eval_jaxpr/gather | solution.py:77
  232.1 10.3 %fusion.88 = (bf16[4,1536,512]{2,1,0:T(8,128)(2,1)}, bf16[4,1536,512]{2,1,0:T(8,128)(2,1)}) fusion(bf16[4,1536,1024]{2,1,0:T(8,128)(2,1)} %bitcast.69), kind=kLoop, calls=%fused_computation.85.clone.1 | loop fusion | bytes 25165824 | tf_op jit(solution)/shard_map/while/body/eval_jaxpr/slice | solution.py:79
  242.4 8.6 %copy.43 = bf16[4,1536,512]{1,2,0:T(8,128)(2,1)} copy(bf16[4,1536,512]{2,1,0:T(8,128)(2,1)} %get-tuple-element.133) | data formatting | bytes 12582912 | tf_op jit(solution)/shard_map/while
  251.0 1.1 constant_dynamic-slice_fusion.3
  252.1 0.3 copy.42
  252.4 0.1 broadcast_compare_fusion.2
  252.4 9.8 %fusion.90 = f32[4,8,128]{2,1,0:T(8,128)S(1)} fusion(pred[4,1536]{1,0:T(4,128)(4,1)S(1)} %broadcast_compare_fusion.2, bf16[4,128,8,64]{1,3,2,0:T(8,128)(2,1)S(1)} %bitcast.74, bf16[4,1536,8,64]{1,3,2,0:T(8,128)(2,1)} %bitcast.70), kind=kOutput, calls=%fused_computation.86.clone.1 | convolution fusion | flops 830473728 | bytes 6838272 | tf_op jit(solution)/shard_map/while/body/eval_jaxpr/sub | solution.py:87
  262.3 14.5 %fusion.91 = f32[4,8,128,1536]{3,2,1,0:T(8,128)} fusion(bf16[4,128,8,64]{1,3,2,0:T(8,128)(2,1)S(1)} %bitcast.75, bf16[4,1536,8,64]{1,3,2,0:T(8,128)(2,1)} %bitcast.71), kind=kOutput, calls=%fused_computation.88.clone.1 | convolution fusion | flops 805306368 | bytes 31981568 | tf_op jit(solution)/shard_map/while/body/eval_jaxpr/gqhd,gkhd->ghqk/dot_general | solution.py:81
  276.8 8.6 %copy.41 = bf16[4,1536,512]{1,2,0:T(8,128)(2,1)} copy(bf16[4,1536,512]{2,1,0:T(8,128)(2,1)} %get-tuple-element.132) | data formatting | bytes 12582912 | tf_op jit(solution)/shard_map/while
  285.4 14.1 %fusion.92 = bf16[4,8,64,128]{3,2,1,0:T(8,128)(2,1)S(1)} fusion(bf16[4,1536,8,64]{1,3,2,0:T(8,128)(2,1)} %bitcast.73, f32[4,8,128]{2,1,0:T(8,128)S(1)} %fusion.90, f32[4,8,128,1536]{3,2,1,0:T(8,128)} %fusion.91, pred[4,1536]{1,0:T(4,128)(4,1)S(1)} %broadcast_compare_fusion.2), kind=kOutput, calls=%fused_computation.12.clone.1 | convolution fusion | flops 837031424 | bytes 32004096 | tf_op jit(solution)/shard_map/while/body/eval_jaxpr/ghqk,gkhd->gqhd/dot_general | solution.py:89
  299.5 0.2 copy.44
  299.8 0.8 constant_dynamic-update-slice_fusion.2
  300.6 2.5 fusion.56
  303.1 1.3 copy-done.4
  304.4 0.4 multiply_reduce_fusion
  304.9 0.0 copy-done
  304.9 0.0 copy-done.9
  304.9 8.6 %add_convert_fusion = bf16[1024,512]{1,0:T(8,128)(2,1)} fusion(f32[1024,512]{1,0:T(8,128)} %copy-done.4, bf16[2048,512]{1,0:T(8,128)(2,1)S(1)} %copy-done, bf16[512,2048]{1,0:T(8,128)(2,1)} %param.22, f32[512]{0:T(512)S(1)} %copy-done.9, f32[1024]{0:T(1024)S(1)} %add_rsqrt_fusion, f32[1024]{0:T(1024)S(1)} %broadcast_multiply_fusion), kind=kOutput, calls=%fused_computation.53 | convolution fusion | flops 4316987392 | bytes 7350272 | tf_op jit(solution)/shard_map/dot_general | solution.py:98
  (20 shorter events, 0.1 us)
Async XLA Ops:
  0.0 304.9 %copy-start = (bf16[2048,512]{1,0:T(8,128)(2,1)S(1)}, bf16[2048,512]{1,0:T(8,128)(2,1)}, u32[]{:S(2)}) copy-start(bf16[2048,512]{1,0:T(8,128)(2,1)} %param.23) | copy-start | bytes 6291460
  0.0 5.0 %copy-start.7 = (bf16[512,512]{1,0:T(8,128)(2,1)S(1)}, bf16[512,512]{1,0:T(8,128)(2,1)}, u32[]{:S(2)}) copy-start(bf16[512,512]{1,0:T(8,128)(2,1)} %param.19) | copy-start | bytes 1572868
  0.0 5.7 %copy-start.8 = (bf16[512,512]{1,0:T(8,128)(2,1)S(1)}, bf16[512,512]{1,0:T(8,128)(2,1)}, u32[]{:S(2)}) copy-start(bf16[512,512]{1,0:T(8,128)(2,1)} %param.18) | copy-start | bytes 1572868
  12.0 105.8 %copy-start.6 = (s32[4,2]{0,1:T(2,128)S(1)}, s32[4,2]{0,1:T(2,128)}, u32[]{:S(2)}) copy-start(s32[4,2]{0,1:T(2,128)} %param.15) | copy-start | bytes 100
  12.0 106.0 %copy-start.5 = (s32[4,2,12]{2,1,0:T(2,128)S(1)}, s32[4,2,12]{2,1,0:T(2,128)}, u32[]{:S(2)}) copy-start(s32[4,2,12]{2,1,0:T(2,128)} %param.14) | copy-start | bytes 1156
  12.0 93.3 %collective-permute-start = (bf16[4,2,128,1024]{3,2,1,0:T(8,128)(2,1)}, bf16[4,2,128,1024]{3,2,1,0:T(8,128)(2,1)S(1)}, u32[]{:S(2)}, u32[]{:S(2)}) collective-permute-start(bf16[4,2,128,1024]{3,2,1,0:T(8,128)(2,1)} %bitcast.76), channel_id=1, source_target_pairs={{0,1},{1,2},{2,3},{3,4},{4,5},{5,6},{6,7},{7,8},{8,9},{9,10},{10,1... | collective-permute-start | bytes 6291464 | tf_op jit(solution)/shard_map/ppermute | solution.py:15
  15.2 93.7 %collective-permute-start.1 = (bf16[4,2,128,1024]{3,2,1,0:T(8,128)(2,1)}, bf16[4,2,128,1024]{3,2,1,0:T(8,128)(2,1)S(1)}, u32[]{:S(2)}, u32[]{:S(2)}) collective-permute-start(bf16[4,2,128,1024]{3,2,1,0:T(8,128)(2,1)} %bitcast.77), channel_id=1, source_target_pairs={{0,15},{1,0},{2,1},{3,2},{4,3},{5,4},{6,5},{7,6},{8,7},{9,8},{10,9... | collective-permute-start | bytes 6291464 | tf_op jit(solution)/shard_map/ppermute | solution.py:15
  105.3 6.9 %copy-start.2 = (bf16[4,2,128,1024]{3,2,1,0:T(8,128)(2,1)}, bf16[4,2,128,1024]{3,2,1,0:T(8,128)(2,1)S(1)}, u32[]{:S(2)}) copy-start(bf16[4,2,128,1024]{3,2,1,0:T(8,128)(2,1)S(1)} %collective-permute-done) | copy-start | bytes 6291460
  108.9 3.3 %copy-start.3 = (bf16[4,2,128,1024]{3,2,1,0:T(8,128)(2,1)}, bf16[4,2,128,1024]{3,2,1,0:T(8,128)(2,1)S(1)}, u32[]{:S(2)}) copy-start(bf16[4,2,128,1024]{3,2,1,0:T(8,128)(2,1)S(1)} %collective-permute-done.1) | copy-start | bytes 6291460
  112.2 22.1 %collective-permute-start.2 = (bf16[1,6,128,1024]{3,2,1,0:T(8,128)(2,1)}, bf16[1,6,128,1024]{3,2,1,0:T(8,128)(2,1)}, u32[]{:S(2)}, u32[]{:S(2)}) collective-permute-start(bf16[1,6,128,1024]{3,2,1,0:T(8,128)(2,1)} %get-tuple-element.89), channel_id=1, source_target_pairs={{0,16},{16,32},{32,48},{48,64},{64,80},{80,96},{96,112},{112,128},... | collective-permute-start | bytes 4718600 | tf_op jit(solution)/shard_map/ppermute | solution.py:21
  114.1 21.9 %collective-permute-start.3 = (bf16[1,6,128,1024]{3,2,1,0:T(8,128)(2,1)}, bf16[1,6,128,1024]{3,2,1,0:T(8,128)(2,1)}, u32[]{:S(2)}, u32[]{:S(2)}) collective-permute-start(bf16[1,6,128,1024]{3,2,1,0:T(8,128)(2,1)} %get-tuple-element.90), channel_id=1, source_target_pairs={{16,0},{32,16},{48,32},{64,48},{80,64},{96,80},{112,96},{128,112},... | collective-permute-start | bytes 4718600 | tf_op jit(solution)/shard_map/ppermute | solution.py:21
  118.0 18.0 %copy-start.1 = (bf16[1024,1024]{1,0:T(8,128)(2,1)S(1)}, bf16[1024,1024]{1,0:T(8,128)(2,1)}, u32[]{:S(2)}) copy-start(bf16[1024,1024]{1,0:T(8,128)(2,1)} %copy.31) | copy-start | bytes 6291460
  300.6 4.3 %copy-start.9 = (f32[512]{0:T(512)S(1)}, f32[512]{0:T(512)}, u32[]{:S(2)}) copy-start(f32[512]{0:T(512)} %param.21) | copy-start | bytes 6148
  303.1 1.4 copy-start.4
where the time goes:
time: 318 us; the launch traced here: 313 us
  waiting for transfers between devices  103 us (32%)
  matrix products  92.5 us (29%)
  local copies, waits for them, and re-layouts  85.6 us (27%)
  other arithmetic  17.6 us (6%)
  starting transfers between devices  14.1 us (4%)
    ppermute x2, waiting for transfers between devices, from_behind(): return lax.ppermute(value, axis, pairs)  88.4 us
    while x4, local copies, waits for them, and re-layouts  34.5 us
    dot_general x2, matrix products, attend_group(): jnp.einsum('gqhd,gkhd->ghqk', qh, kh, preferred_element_type=jnp.float32)  29.1 us
    dot_general x2, matrix products, attend_group(): jnp.einsum('ghqk,gkhd->gqhd', weights, vh, preferred_element_type=jnp.flo...  28.2 us
    slice x2, local copies, waits for them, and re-layouts, attend_group(): kh = gathered[..., :width].reshape(group, nkeys, HEADS, head_dim)  20.6 us
    gather x2, local copies, waits for them, and re-layouts, attend_group(): gathered = extended[ig].reshape(group, nkeys, 2 * width)  20.1 us
    sub x2, matrix products, attend_group(): expo = jnp.exp(scores - top)  19.6 us
    ppermute x2, waiting for transfers between devices, passed_along(): return lax.ppermute(value, axis, pairs)  15.1 us
  transfers between devices with their start and end apart: 4, of which 4 were waited for; matrix products, arithmetic and copies ran while one was open for 1% of the time, Pallas kernels for 0%

commit v1 on v0

v1 whole, which is shorter than its diff:
```python
import math

import jax
import jax.numpy as jnp
from jax import lax
from jax.experimental import pallas as pl
from jax.experimental.pallas import tpu as pltpu
from jax.sharding import PartitionSpec as P

HEADS = 8
NBR = 12
NULL = 36
AXES = ("lat", "lon")
F32 = jnp.float32
BF16 = jnp.bfloat16
NT = (((1,), (1,)), ((), ()))


def moved(value, target):
    lats, lons = lax.axis_size("lat"), lax.axis_size("lon")
    pairs = []
    for la in range(lats):
        for lo in range(lons):
            to = target(la, lo)
            if to is not None:
                pairs.append((la * lons + lo, to[0] * lons + to[1]))
    return lax.ppermute(value, AXES, pairs)


def to_partner(value):
    return moved(value, lambda la, lo: (la, lo ^ 1))


def along_z(value):
    lons = lax.axis_size("lon")
    return moved(value, lambda la, lo: (la, (lo + (2 if lo % 2 == 0 else -2)) % lons))


def to_next_lat(value):
    lats = lax.axis_size("lat")
    return moved(value, lambda la, lo: (la + 1, lo) if la + 1 < lats else None)


def to_last_lat(value):
    return moved(value, lambda la, lo: (la - 1, lo) if la > 0 else None)


def slots_of(neighbours, live, rows, cols):
    total_lon = cols * lax.axis_size("lon")
    lat = lax.axis_index("lat")
    lon = lax.axis_index("lon")
    dr = neighbours // total_lon - lat * rows
    dc = (neighbours % total_lon - lon * cols + 2) % total_lon
    side = jnp.where(dc < 2, 0, 1)
    partner_side = jnp.where(lon % 2 == 0, 1, 0)
    kind = jnp.where((dc == 2) | (dc == 3), 0, jnp.where(side == partner_side, 1, 2))
    col = dc % 2
    place = jnp.where(dr == 0, 0, jnp.where(dr == 3, 1, dr + 1))
    place = jnp.where(kind == 0, dr, place)
    inner = kind * 8 + place * 2 + col
    edge = kind * 2 + col
    slot = jnp.where(dr < 0, 24 + edge, jnp.where(dr >= rows, 30 + edge, inner))
    usable = jnp.arange(NBR, dtype=jnp.int32) < live[..., None]
    slot = jnp.where(usable, jnp.clip(slot, 0, NULL), NULL)
    return slot.reshape(rows * cols, NBR)


def normalize(x, gain):
    centre = x - jnp.mean(x, axis=-1, keepdims=True)
    spread = jnp.mean(centre * centre, axis=-1, keepdims=True)
    return centre * lax.rsqrt(spread + 1e-05) * gain


def dot(a, b):
    return jnp.dot(a, b, preferred_element_type=F32)


def layer_kernel(
    slots, counts,
    own, par_o, par_i, far_o, far_i, up, down,
    gain_attn, wq_t, wk, wv_t, wo, gain_mlp, w_in, w_back,
    out,
    kscr, vscr, qscr, att, chk,
):
    pairs_all = (
        (own, 0, 4), (par_o, 8, 2), (par_i, 12, 2), (far_o, 16, 2), (far_i, 20, 2),
        (up, 24, 3), (down, 30, 3),
    )
    kscr[NULL] = jnp.zeros((128, 512), BF16)
    vscr[NULL] = jnp.zeros((4, 144, 128), BF16)
    chk[...] = jnp.zeros_like(chk)
    zeros = jnp.zeros((64, 128), BF16)

    for src, base, n in pairs_all:
        def project(i, carry, src=src, base=base):
            at = base + 2 * i
            x = src[pl.ds(2 * i, 2)].astype(F32).reshape(256, 512)
            y = normalize(x, gain_attn[...]).astype(BF16)
            k = dot(y, wk[...]).astype(BF16)
            kscr[at] = k[:128]
            kscr[at + 1] = k[128:]
            vt = lax.dot_general(wv_t[...], y, NT, preferred_element_type=F32).astype(BF16)
            for blk in range(2):
                for hp in range(4):
                    vscr[at + blk, hp, pl.ds(0, 128)] = vt[hp * 128:(hp + 1) * 128, blk * 128:(blk + 1) * 128]
                    vscr[at + blk, hp, pl.ds(128, 16)] = jnp.ones((16, 128), BF16)
            if src is own:
                qt = lax.dot_general(wq_t[...], y, NT, preferred_element_type=F32).astype(BF16)
                qt = (qt * 0.125).astype(BF16)
                for blk in range(2):
                    for hp in range(4):
                        h0 = qt[hp * 128:hp * 128 + 64, blk * 128:(blk + 1) * 128]
                        h1 = qt[hp * 128 + 64:(hp + 1) * 128, blk * 128:(blk + 1) * 128]
                        qscr[at + blk, hp, pl.ds(0, 64)] = jnp.concatenate([h0, zeros], axis=1)
                        qscr[at + blk, hp, pl.ds(64, 64)] = jnp.concatenate([zeros, h1], axis=1)
            return carry
        lax.fori_loop(0, n, project, 0)

    def finish(o, den):
        inv = 1.0 / den
        h0 = o[0:64, 0:128] * inv[:, 0:128]
        h1 = o[64:128, 128:256] * inv[:, 128:256]
        return jnp.concatenate([h0, h1], axis=0)

    def attend(b, carry):
        ids = [slots[b, n] for n in range(NBR)]
        parts = []
        bad = jnp.zeros((1, 256), F32)
        for hp in range(4):
            q = qscr[b, hp]
            keys = jnp.concatenate([kscr[i, :, hp * 128:(hp + 1) * 128] for i in ids], axis=0)
            p = jnp.exp(dot(keys, q)).astype(BF16)
            vals = jnp.concatenate([vscr[i, hp] for i in ids], axis=1)
            o = dot(vals, p)
            den = o[128:129]
            good = (den > 2.0 ** -60) & (den < 2.0 ** 100)
            bad = jnp.maximum(bad, jnp.where(good, 0.0, 1.0))
            parts.append(finish(o, den))
        chk[...] = jnp.maximum(chk[...], bad)
        full = jnp.concatenate(parts, axis=0)
        att[pl.ds(pl.multiple_of(b * 128, 128), 128)] = full.T.astype(BF16)
        return carry

    lax.fori_loop(0, 8, attend, 0)

    @pl.when(jnp.max(chk[...]) > 0.5)
    def _():
        def attend_shifted(b, carry):
            parts = []
            for hp in range(4):
                q = qscr[b, hp]

                def scores(n, hp=hp, q=q):
                    return dot(kscr[slots[b, n], :, hp * 128:(hp + 1) * 128], q)

                def top_of(n, m):
                    return jnp.maximum(m, jnp.max(scores(n), axis=0, keepdims=True))

                top = lax.fori_loop(0, counts[b], top_of, jnp.full((1, 256), -3e38, F32))

                def add(n, o, hp=hp, top=top):
                    p = jnp.exp(scores(n) - top).astype(BF16)
                    return o + dot(vscr[slots[b, n], hp], p)

                o = lax.fori_loop(0, counts[b], add, jnp.zeros((144, 256), F32))
                parts.append(finish(o, o[128:129]))
            full = jnp.concatenate(parts, axis=0)
            att[pl.ds(pl.multiple_of(b * 128, 128), 128)] = full.T.astype(BF16)
            return carry

        lax.fori_loop(0, 8, attend_shifted, 0)

    def mlp(i, carry):
        x = own[pl.ds(2 * i, 2)].astype(F32).reshape(256, 512)
        a = att[pl.ds(pl.multiple_of(i * 256, 256), 256)]
        mid = x + dot(a, wo[...])
        y = normalize(mid, gain_mlp[...]).astype(BF16)
        inner = jax.nn.gelu(dot(y, w_in[...]), approximate=True).astype(BF16)
        res = mid + dot(inner, w_back[...])
        out[pl.ds(2 * i, 2)] = res.astype(BF16).reshape(2, 128, 512)
        return carry

    lax.fori_loop(0, 4, mlp, 0)


def shards(
    nodes, neighbours, live, gain_attn, w_query, w_key, w_value, w_out, gain_mlp, w_in, w_back
):
    rows, cols, nblk, width = nodes.shape
    blocks = rows * cols
    outer = jnp.concatenate([nodes[:1], nodes[3:]], axis=0)
    par_o = to_partner(outer)
    par_i = to_partner(nodes[1:3])
    far_o = along_z(par_o)
    far_i = along_z(par_i)
    down_row = jnp.concatenate([nodes[3], par_o[1], far_o[1]], axis=0)
    up_row = jnp.concatenate([nodes[0], par_o[0], far_o[0]], axis=0)
    up = to_next_lat(down_row)
    down = to_last_lat(up_row)
    slots = slots_of(neighbours, live, rows, cols)
    flat = lambda v: v.reshape(-1, nblk, width)
    smem = pl.BlockSpec(memory_space=pltpu.SMEM)
    vmem = pl.BlockSpec(memory_space=pltpu.VMEM)
    result = pl.pallas_call(
        layer_kernel,
        out_shape=jax.ShapeDtypeStruct((blocks, nblk, width), BF16),
        in_specs=[smem, smem] + [vmem] * 15,
        out_specs=vmem,
        scratch_shapes=[
            pltpu.VMEM((NULL + 1, 128, 512), BF16),
            pltpu.VMEM((NULL + 1, 4, 144, 128), BF16),
            pltpu.VMEM((8, 4, 128, 256), BF16),
            pltpu.VMEM((1024, 512), BF16),
            pltpu.VMEM((1, 256), F32),
        ],
        compiler_params=pltpu.CompilerParams(vmem_limit_bytes=56 * 2**20),
    )(
        slots, live.reshape(blocks),
        flat(nodes), flat(par_o), flat(par_i), flat(far_o), flat(far_i), up, down,
        gain_attn.reshape(1, width), w_query.T, w_key, w_value.T, w_out, gain_mlp.reshape(1, width), w_in, w_back,
    )
    return result.reshape(rows, cols, nblk, width)


def solution(mesh):
    placed = (
        P("lat", "lon", None, None),
        P("lat", "lon", None),
        P("lat", "lon"),
        P(), P(), P(), P(), P(), P(), P(), P(),
    )
    return jax.shard_map(
        shards, mesh=mesh, in_specs=placed, out_specs=P("lat", "lon", None, None), check_vma=False
    )
```

time: 318 us -> 278 us (0.87); the launches traced: 313 us -> 280 us
  Pallas kernels: 0 us -> 224 us
  matrix products: 92.5 us -> 0 us
  local copies, waits for them, and re-layouts: 85.6 us -> 4.96 us
  waiting for transfers between devices: 103 us -> 31.4 us
  other arithmetic: 17.6 us -> 0.9 us
  starting transfers between devices: 14.1 us -> 18.2 us
    pallas_call x0 -> x1, Pallas kernels: none -> 224 us  [shards(): pl.pallas_call(layer_kernel, out_shape=jax.ShapeDtypeStruct((blocks, nblk...]
    dot_general x9 -> x0, matrix products: 72.8 us -> none  [the longest x2 29.1 us: attend_group(): jnp.einsum('gqhd,gkhd->ghqk', qh, kh, preferred_element_type=jnp.float32)]
    ppermute x4 -> x6, waiting for transfers between devices: 103 us -> 31.4 us  [moved(): return lax.ppermute(value, AXES, pairs)]
    while x4 -> x0, local copies, waits for them, and re-layouts: 34.5 us -> none
    slice x2 -> x1, local copies, waits for them, and re-layouts: 20.6 us -> 0.03 us  [shards(): par_i = to_partner(nodes[1:3])]
    gather x2 -> x0, local copies, waits for them, and re-layouts: 20.1 us -> none  [attend_group(): gathered = extended[ig].reshape(group, nkeys, 2 * width)]
    sub x2 -> x0, matrix products: 19.6 us -> none  [attend_group(): expo = jnp.exp(scores - top)]
    concatenate x2 -> x3, other arithmetic: 8.74 us -> 0.23 us  [the longest x1 0.09 us: shards(): down_row = jnp.concatenate([nodes[3], par_o[1], far_o[1]], axis=0)]
  transfers between devices with their start and end apart: 4 -> 6, of which waited for: 4 -> 3; matrix products, arithmetic and copies ran while one was open for 1% -> 1% of each run, Pallas kernels for 0% -> 0%
where the time goes in v1:
time: 278 us; the launch traced here: 280 us
  Pallas kernels  224 us (81%)
  waiting for transfers between devices  31.4 us (11%)
  starting transfers between devices  18.2 us (7%)
  local copies, waits for them, and re-layouts  4.96 us (2%)
    pallas_call x1, Pallas kernels, shards(): pl.pallas_call(layer_kernel, out_shape=jax.ShapeDtypeStruct((blocks, nblk...  224 us
    ppermute x6, waiting for transfers between devices, moved(): return lax.ppermute(value, AXES, pairs)  31.4 us
    ppermute x6, starting transfers between devices, moved(): return lax.ppermute(value, AXES, pairs)  18.2 us
  transfers between devices with their start and end apart: 6, of which 3 were waited for; matrix products, arithmetic and copies ran while one was open for 1% of the time, Pallas kernels for 0%

profile of v1, /device:TPU:6, one launch (start us, length us, event | category | flops | bytes accessed | tf_op | source)
XLA Modules:
  0.0 279.8 jit_solution(7889302916340676443)
XLA Ops:
  0.0 0.0 copy-start
  0.0 1.2 slice_bitcast_fusion.5
  1.2 0.1 pad_maximum_fusion.2
  1.3 3.3 %collective-permute-start = (bf16[2,2,128,512]{3,2,1,0:T(8,128)(2,1)S(1)}, bf16[2,2,128,512]{3,2,1,0:T(8,128)(2,1)S(1)}, u32[]{:S(2)}, u32[]{:S(2)}) collective-permute-start(bf16[2,2,128,512]{3,2,1,0:T(8,128)(2,1)S(1)} %pad_maximum_fusion.2), channel_id=1, source_target_pairs={{0,1},{1,0},{2,3},{3,2},{4,5},{5,4},{6,7},{7,6},{8,9},{9,8},{10,11... | collective-permute-start | bytes 1572872 | tf_op jit(solution)/shard_map/ppermute | solution.py:27
  4.6 12.0 %collective-permute-done = bf16[2,2,128,512]{3,2,1,0:T(8,128)(2,1)S(1)} collective-permute-done((bf16[2,2,128,512]{3,2,1,0:T(8,128)(2,1)S(1)}, bf16[2,2,128,512]{3,2,1,0:T(8,128)(2,1)S(1)}, u32[]{:S(2)}, u32[]{:S(2)}) %collective-permute-start) | collective-permute-done | bytes 524320 | tf_op jit(solution)/shard_map/ppermute | solution.py:27
  16.5 0.0 copy-start.1
  16.5 1.9 collective-permute-start.2
  18.4 0.0 copy-done
  18.5 7.2 %collective-permute-start.1 = (bf16[2,2,128,512]{3,2,1,0:T(8,128)(2,1)S(1)}, bf16[2,2,128,512]{3,2,1,0:T(8,128)(2,1)}, u32[]{:S(2)}, u32[]{:S(2)}) collective-permute-start(bf16[2,2,128,512]{3,2,1,0:T(8,128)(2,1)S(1)} %slice.25), channel_id=1, source_target_pairs={{0,1},{1,0},{2,3},{3,2},{4,5},{5,4},{6,7},{7,6},{8,9},{9,8},{10,11... | collective-permute-start | bytes 1572872 | tf_op jit(solution)/shard_map/ppermute | solution.py:27
  25.7 0.0 copy-start.7
  25.8 0.0 copy-start.4
  25.8 7.7 %collective-permute-done.2 = bf16[2,2,128,512]{3,2,1,0:T(8,128)(2,1)S(1)} collective-permute-done((bf16[2,2,128,512]{3,2,1,0:T(8,128)(2,1)S(1)}, bf16[2,2,128,512]{3,2,1,0:T(8,128)(2,1)S(1)}, u32[]{:S(2)}, u32[]{:S(2)}) %collective-permute-start.2) | collective-permute-done | bytes 524320 | tf_op jit(solution)/shard_map/ppermute | solution.py:27
  33.4 0.0 copy-start.2
  33.5 0.0 copy-start.5
  33.5 0.1 pad_maximum_fusion
  33.6 0.0 copy-done.1
  33.6 0.0 copy-start.6
  33.6 2.1 collective-permute-start.4
  35.7 0.1 pad_maximum_fusion.1
  35.8 0.0 copy-done.2
  35.8 3.6 %collective-permute-start.5 = (bf16[6,128,512]{2,1,0:T(8,128)(2,1)S(1)}, bf16[6,128,512]{2,1,0:T(8,128)(2,1)}, u32[]{:S(2)}, u32[]{:S(2)}) collective-permute-start(bf16[6,128,512]{2,1,0:T(8,128)(2,1)S(1)} %pad_maximum_fusion.1), channel_id=1, source_target_pairs={{16,0},{17,1},{18,2},{19,3},{20,4},{21,5},{22,6},{23,7},{24,8},{25... | collective-permute-start | bytes 2359304 | tf_op jit(solution)/shard_map/ppermute | solution.py:27
  39.4 0.0 collective-permute-done.1
  39.4 0.1 collective-permute-start.3
  39.5 0.0 copy-done.7
  39.6 0.1 copy.16
  39.6 0.6 reshape.32.counts
  40.2 0.0 copy-done.4
  40.2 1.0 copy.18
  41.3 0.0 copy-done.5
  41.3 1.0 copy.19
  42.3 0.0 copy-done.6
  42.3 0.7 compare_select_fusion.11
  43.0 11.8 %collective-permute-done.3 = bf16[2,2,128,512]{3,2,1,0:T(8,128)(2,1)} collective-permute-done((bf16[2,2,128,512]{3,2,1,0:T(8,128)(2,1)}, bf16[2,2,128,512]{3,2,1,0:T(8,128)(2,1)}, u32[]{:S(2)}, u32[]{:S(2)}) %collective-permute-start.3) | collective-permute-done | bytes 524320 | tf_op jit(solution)/shard_map/ppermute | solution.py:27
  54.7 0.0 collective-permute-done.4.up
  54.7 0.0 copy-start.3
  54.7 0.0 collective-permute-done.5.down
  54.8 0.9 copy-done.3
  55.6 224.2 %shard_map.109 = bf16[8,128,512]{2,1,0:T(8,128)(2,1)} custom-call(s32[8,12]{1,0:T(8,128)} %bitcast.28, s32[8]{0:T(128)} %reshape.32.counts, bf16[8,128,512]{2,1,0:T(8,128)(2,1)} %bitcast.23, bf16[4,128,512]{2,1,0:T(8,128)(2,1)} %bitcast.24, bf16[4,128,512]{2,1,0:T(8,128)(2,1)} %bitcast.3.par_i, bf16[4,128,512]{2,1,0:T(8,128)(2,1)} %bitcast.25, ...), custom_call_target="tpu_custom_call" | custom-call | tf_op jit(solution)/shard_map/pallas_call | solution.py:204
  (3 shorter events, 0.1 us)
Async XLA Ops:
  0.0 18.4 %copy-start = (bf16[4,2,128,512]{3,2,1,0:T(8,128)(2,1)S(1)}, bf16[4,2,128,512]{3,2,1,0:T(8,128)(2,1)}, u32[]{:S(2)}) copy-start(bf16[4,2,128,512]{3,2,1,0:T(8,128)(2,1)} %param.11) | copy-start | bytes 3145732
  1.3 15.3 %collective-permute-start = (bf16[2,2,128,512]{3,2,1,0:T(8,128)(2,1)S(1)}, bf16[2,2,128,512]{3,2,1,0:T(8,128)(2,1)S(1)}, u32[]{:S(2)}, u32[]{:S(2)}) collective-permute-start(bf16[2,2,128,512]{3,2,1,0:T(8,128)(2,1)S(1)} %pad_maximum_fusion.2), channel_id=1, source_target_pairs={{0,1},{1,0},{2,3},{3,2},{4,5},{5,4},{6,7},{7,6},{8,9},{9,8},{10,11... | collective-permute-start | bytes 1572872 | tf_op jit(solution)/shard_map/ppermute | solution.py:27
  16.5 17.1 %copy-start.1 = (bf16[2,2,128,512]{3,2,1,0:T(8,128)(2,1)}, bf16[2,2,128,512]{3,2,1,0:T(8,128)(2,1)S(1)}, u32[]{:S(2)}) copy-start(bf16[2,2,128,512]{3,2,1,0:T(8,128)(2,1)S(1)} %collective-permute-done) | copy-start | bytes 1572868
  16.5 16.9 %collective-permute-start.2 = (bf16[2,2,128,512]{3,2,1,0:T(8,128)(2,1)S(1)}, bf16[2,2,128,512]{3,2,1,0:T(8,128)(2,1)S(1)}, u32[]{:S(2)}, u32[]{:S(2)}) collective-permute-start(bf16[2,2,128,512]{3,2,1,0:T(8,128)(2,1)S(1)} %collective-permute-done), channel_id=1, source_target_pairs={{0,2},{1,15},{2,4},{3,1},{4,6},{5,3},{6,8},{7,5},{8,10},{9,7},{10,... | collective-permute-start | bytes 1572872 | tf_op jit(solution)/shard_map/ppermute | solution.py:27
  18.5 20.9 %collective-permute-start.1 = (bf16[2,2,128,512]{3,2,1,0:T(8,128)(2,1)S(1)}, bf16[2,2,128,512]{3,2,1,0:T(8,128)(2,1)}, u32[]{:S(2)}, u32[]{:S(2)}) collective-permute-start(bf16[2,2,128,512]{3,2,1,0:T(8,128)(2,1)S(1)} %slice.25), channel_id=1, source_target_pairs={{0,1},{1,0},{2,3},{3,2},{4,5},{5,4},{6,7},{7,6},{8,9},{9,8},{10,11... | collective-permute-start | bytes 1572872 | tf_op jit(solution)/shard_map/ppermute | solution.py:27
  25.7 13.8 %copy-start.7 = (s32[4,2]{0,1:T(2,128)S(1)}, s32[4,2]{0,1:T(2,128)}, u32[]{:S(2)}) copy-start(s32[4,2]{0,1:T(2,128)} %param.13) | copy-start | bytes 100
  25.8 14.5 %copy-start.4 = (bf16[512,512]{1,0:T(8,128)(2,1)S(1)}, bf16[512,512]{1,0:T(8,128)(2,1)}, u32[]{:S(2)}) copy-start(bf16[512,512]{1,0:T(8,128)(2,1)} %param.15) | copy-start | bytes 1572868
  33.4 2.3 copy-start.2
  33.5 7.8 %copy-start.5 = (bf16[512,512]{1,0:T(8,128)(2,1)S(1)}, bf16[512,512]{1,0:T(8,128)(2,1)}, u32[]{:S(2)}) copy-start(bf16[512,512]{1,0:T(8,128)(2,1)} %param.17) | copy-start | bytes 1572868
  33.6 8.7 %copy-start.6 = (s32[4,2,12]{2,1,0:T(2,128)S(1)}, s32[4,2,12]{2,1,0:T(2,128)}, u32[]{:S(2)}) copy-start(s32[4,2,12]{2,1,0:T(2,128)} %param.12) | copy-start | bytes 1156
  33.6 21.1 %collective-permute-start.4 = (bf16[6,128,512]{2,1,0:T(8,128)(2,1)S(1)}, bf16[6,128,512]{2,1,0:T(8,128)(2,1)S(1)}, u32[]{:S(2)}, u32[]{:S(2)}) collective-permute-start(bf16[6,128,512]{2,1,0:T(8,128)(2,1)S(1)} %pad_maximum_fusion), channel_id=1, source_target_pairs={{0,16},{1,17},{2,18},{3,19},{4,20},{5,21},{6,22},{7,23},{8,24},{9,... | collective-permute-start | bytes 2359304 | tf_op jit(solution)/shard_map/ppermute | solution.py:27
  35.8 19.0 %collective-permute-start.5 = (bf16[6,128,512]{2,1,0:T(8,128)(2,1)S(1)}, bf16[6,128,512]{2,1,0:T(8,128)(2,1)}, u32[]{:S(2)}, u32[]{:S(2)}) collective-permute-start(bf16[6,128,512]{2,1,0:T(8,128)(2,1)S(1)} %pad_maximum_fusion.1), channel_id=1, source_target_pairs={{16,0},{17,1},{18,2},{19,3},{20,4},{21,5},{22,6},{23,7},{24,8},{25... | collective-permute-start | bytes 2359304 | tf_op jit(solution)/shard_map/ppermute | solution.py:27
  39.4 15.3 %collective-permute-start.3 = (bf16[2,2,128,512]{3,2,1,0:T(8,128)(2,1)}, bf16[2,2,128,512]{3,2,1,0:T(8,128)(2,1)}, u32[]{:S(2)}, u32[]{:S(2)}) collective-permute-start(bf16[2,2,128,512]{3,2,1,0:T(8,128)(2,1)} %collective-permute-done.1), channel_id=1, source_target_pairs={{0,2},{1,15},{2,4},{3,1},{4,6},{5,3},{6,8},{7,5},{8,10},{9,7},{10,... | collective-permute-start | bytes 1572872 | tf_op jit(solution)/shard_map/ppermute | solution.py:27
  54.7 0.9 copy-start.3
